TPU v7x, 32 devices: a whole 2x2x4 slice. The times are simulated.
32 devices in a mesh: head: 2 (over y), ctx: 16 (over z, x, core).
Axes of the slice: x: 2, y: 2, z: 4, core: 2. Of those that a mesh axis runs over, the one named last changes fastest.
Arguments:
- queries: bfloat16 [8192, 64, 128], P(('ctx', 'head')), may hold values from -6 to 6
- keys: bfloat16 [8192, 8, 128], P(('ctx', 'head')), may hold values from -6 to 6
- values: bfloat16 [8192, 8, 128], P(('ctx', 'head')), may hold values from -6 to 6
- out_grad: bfloat16 [8192, 64, 128], P(('ctx', 'head')), may hold values from -6 to 6
- doc_lengths: int32 [48], replicated, may hold values from 1 to 1024, 8192 in all
- stored_block_order: int32 [64], replicated, may hold values from 0 to 63, as said below
Outputs:
- attended: bfloat16 [8192, 64, 128], P(('ctx', 'head'))
- query_grad: bfloat16 [8192, 64, 128], P(('ctx', 'head'))
- key_gradient: bfloat16 [8192, 8, 128], P(('ctx', 'head'))
- value_gradient: bfloat16 [8192, 8, 128], P(('ctx', 'head'))
Inputs may be any that keep to these rules, and one draw needn't show every extreme that they name: `doc_lengths`: they sum to 8192 and the largest is exactly 1024. A permutation in which stored_block_order[b] // 4 = b // 4: the stored blocks of each aligned group of 4 are that group's sequence blocks in some order.
All inputs are finite; a program needn't handle non-finite values.
Results may differ from a plain program's by a relative error of at most 0.039.
Values may be sent and summed in bfloat16 or wider, within the bound.
A program may use at most 192 MiB of HBM per device.

v0:
```python
import functools
import math

import jax
import jax.numpy as jnp
from jax import lax
from jax.experimental import pallas as pl
from jax.experimental.pallas import tpu as pltpu
from jax.sharding import PartitionSpec as P

HEAD_SIZE = 128
BLOCK_TOKENS = 128
HOPS = 2
DOC_MOST = 1024
CHUNKS = (2, 4, 2)
SIDE = 2
NEG_BIG = -1e30
SCALE = HEAD_SIZE ** (-0.5)
SCALE_LOG2 = SCALE * math.log2(math.e)

NN = (((1,), (0,)), ((), ()))
NT = (((1,), (1,)), ((), ()))
TN = (((0,), (0,)), ((), ()))


def dot(a, b, dims):
    return lax.dot_general(a, b, dims, preferred_element_type=jnp.float32)


def attention_kernel(slot_ref, span_ref, info_ref, q_ref, g_ref, kv_ref, *rest):
    o_ref, dq_ref, dkv_ref = rest[-3 - 5 * SIDE : -5 * SIDE]
    scratch = rest[-5 * SIDE :]
    s_scr, e_scr, out_acc, dq_acc, dkv_acc = (scratch[k * SIDE : (k + 1) * SIDE] for k in range(5))
    turn = pl.program_id(1)
    bt = q_ref.shape[0]
    share = q_ref.shape[1] // SIDE
    rows = bt * share
    sides = range(SIDE)

    @pl.when(turn == 0)
    def _():
        for a in sides:
            dkv_acc[a][...] = jnp.zeros_like(dkv_acc[a])

    last = span_ref[3 * turn]
    tiles = span_ref[3 * turn + 1]
    clean = span_ref[3 * turn + 2]
    query = [q_ref[:, a * share : (a + 1) * share, :].reshape(rows, HEAD_SIZE) for a in sides]
    query_t = [q.T for q in query]
    start = info_ref[0, 0:1, :]
    place = info_ref[0, 1:2, :]

    def slots(t):
        high = last - 2 * t
        return slot_ref[jnp.maximum(high - 1, 0)], slot_ref[high]

    def tile_of(a, which, t):
        low, high = slots(t)
        return jnp.concatenate([kv_ref[a, which, low], kv_ref[a, which, high]], axis=0)

    def fold(x, op):
        return op(x.reshape(2 * bt // 8, 8, rows), axis=0)

    def scores(t, lower, upper):
        found = []
        if lower:
            kpos = (last - 2 * t - 1) * bt + lax.broadcasted_iota(jnp.int32, (2 * bt, 1), 0)
            keep = kpos >= start
            if upper:
                keep = keep & (kpos <= place)
        for a in sides:
            s = dot(tile_of(a, 0, t), query_t[a], NN)
            if lower:
                s = jnp.where(keep, s, NEG_BIG)
            s_scr[a][t] = s
            found.append(fold(s, jnp.max))
        return found

    def larger(lower):
        return lambda t, m: [jnp.maximum(x, y) for x, y in zip(m, scores(t, lower, False))]

    best = scores(0, True, True)
    best = lax.fori_loop(1, clean, larger(False), best)
    best = lax.fori_loop(clean, tiles, larger(True), best)
    top = [jnp.max(m, axis=0, keepdims=True) * SCALE_LOG2 for m in best]

    for a in sides:
        out_acc[a][...] = jnp.zeros_like(out_acc[a])
        dq_acc[a][...] = jnp.zeros_like(dq_acc[a])

    def weights(t, totals):
        new = []
        for a in sides:
            e = jnp.exp2(s_scr[a][t] * SCALE_LOG2 - top[a])
            low = e.astype(jnp.bfloat16)
            e_scr[a][t] = low
            out_acc[a][...] += dot(tile_of(a, 1, t), low, TN)
            new.append(totals[a] + fold(e, jnp.sum))
        return new

    totals = lax.fori_loop(0, tiles, weights, [jnp.zeros((8, rows), jnp.float32)] * SIDE)
    grad_t, grad, delta = [], [], []
    for a in sides:
        inv = 1.0 / jnp.sum(totals[a], axis=0, keepdims=True)
        own = slice(a * share, (a + 1) * share)
        out_t = (out_acc[a][...] * inv).astype(jnp.bfloat16)
        o_ref[:, own, :] = out_t.T.reshape(bt, share, HEAD_SIZE)
        raw = g_ref[:, own, :].reshape(rows, HEAD_SIZE).T
        scaled = (raw.astype(jnp.float32) * inv).astype(jnp.bfloat16)
        product = scaled.astype(jnp.float32) * out_t.astype(jnp.float32)
        delta.append(jnp.sum(product, axis=0, keepdims=True))
        grad_t.append(scaled)
        grad.append(scaled.T)

    def back(t, carry):
        low, high = slots(t)
        for a in sides:
            e = e_scr[a][t]
            dp = dot(tile_of(a, 1, t), grad_t[a], NN)
            ds = (e.astype(jnp.float32) * (dp - delta[a])).astype(jnp.bfloat16)
            dq_acc[a][...] += dot(tile_of(a, 0, t), ds, TN)
            dk = dot(ds, query[a], NN)
            dv = dot(e, grad[a], NN)
            dkv_acc[a][0, low] += dk[:bt]
            dkv_acc[a][0, high] += dk[bt:]
            dkv_acc[a][1, low] += dv[:bt]
            dkv_acc[a][1, high] += dv[bt:]
        return carry

    lax.fori_loop(0, tiles, back, 0)
    for a in sides:
        own = slice(a * share, (a + 1) * share)
        dq = (dq_acc[a][...] * SCALE).astype(jnp.bfloat16)
        dq_ref[:, own, :] = dq.T.reshape(bt, share, HEAD_SIZE)

    @pl.when(turn == pl.num_programs(1) - 1)
    def _():
        for a in sides:
            dkv_ref[a, 0] = (dkv_acc[a][0] * SCALE).astype(jnp.bfloat16)
            dkv_ref[a, 1] = dkv_acc[a][1].astype(jnp.bfloat16)


def attend(slot_of, spans, info, queries, out_grad, window, first_head, so_far):
    tokens, heads, _ = queries.shape
    chunk, _, wblocks = window.shape[:3]
    bt = window.shape[3]
    share = info.shape[2] // bt
    turns = tokens // bt
    rows = bt * share
    max_tiles = DOC_MOST // bt // 2 + 1
    by_head = pl.BlockSpec(
        (bt, SIDE * share, HEAD_SIZE), lambda h, i, *_: (i, first_head // SIDE + h, 0)
    )
    kv_spec = pl.BlockSpec(
        (SIDE, 2, wblocks, bt, HEAD_SIZE), lambda h, i, *_: (h, 0, 0, 0, 0)
    )
    in_specs = [
        pl.BlockSpec((1, 2, rows), lambda h, i, *_: (i, 0, 0)),
        by_head,
        by_head,
        kv_spec,
    ]
    operands = [slot_of, spans, info, queries, out_grad, window]
    aliases = {}
    if so_far is not None:
        in_specs += [pl.BlockSpec(memory_space=pl.ANY)] * 2
        operands += list(so_far)
        aliases = {6: 0, 7: 1}
    big = jax.ShapeDtypeStruct(queries.shape, jnp.bfloat16)
    pairs = chunk * turns * rows * 6 * bt
    return pl.pallas_call(
        attention_kernel,
        grid_spec=pltpu.PrefetchScalarGridSpec(
            num_scalar_prefetch=2,
            grid=(chunk // SIDE, turns),
            in_specs=in_specs,
            out_specs=[by_head, by_head, kv_spec],
            scratch_shapes=[pltpu.VMEM((max_tiles, 2 * bt, rows), jnp.float32)] * SIDE
            + [pltpu.VMEM((max_tiles, 2 * bt, rows), jnp.bfloat16)] * SIDE
            + [pltpu.VMEM((HEAD_SIZE, rows), jnp.float32)] * (2 * SIDE)
            + [pltpu.VMEM((2, wblocks, bt, HEAD_SIZE), jnp.float32)] * SIDE,
        ),
        out_shape=[big, big, jax.ShapeDtypeStruct(window.shape, jnp.bfloat16)],
        input_output_aliases=aliases,
        compiler_params=pltpu.CompilerParams(vmem_limit_bytes=48 * 1024 * 1024),
        cost_estimate=pl.CostEstimate(
            flops=12 * pairs * HEAD_SIZE,
            bytes_accessed=4 * chunk * tokens * share * HEAD_SIZE * 2 + 4 * window.size,
            transcendentals=pairs,
        ),
    )(*operands)


def shifted(block, axis, distance):
    size = lax.axis_size(axis)
    route = [(i - distance, i) for i in range(size) if 0 <= i - distance < size]
    return lax.ppermute(block, axis, route)


def rolled(block, axis, distance):
    size = lax.axis_size(axis)
    return lax.ppermute(block, axis, [(i, (i + distance) % size) for i in range(size)])


def body(queries, keys, values, out_grad, doc_lengths, stored_block_order):
    tokens, heads, _ = queries.shape
    bt = min(BLOCK_TOKENS, tokens)
    pieces = BLOCK_TOKENS // bt
    stored_order = stored_block_order[:, None] * pieces + jnp.arange(pieces, dtype=jnp.int32)
    stored_order = stored_order.reshape(-1)
    kv_heads = keys.shape[1]
    share = heads // kv_heads
    own_blocks = tokens // bt
    split = lax.axis_size("head")
    me_head, me_ctx = lax.axis_index("head"), lax.axis_index("ctx")
    group = own_blocks * split
    window_blocks = (HOPS + 1) * group

    w = jnp.arange(window_blocks, dtype=jnp.int32)
    hop, turn, inner = w // group, (w % group) // own_blocks, w % own_blocks
    source = lax.rem(me_head - turn + split, split)
    stored = jnp.maximum(me_ctx - hop, 0) * group + source * own_blocks + inner
    rel = (HOPS - hop) * group + stored_order[stored] % group
    slot_of = jnp.sum(jnp.where(rel[None, :] == w[:, None], w[None, :], 0), axis=1).astype(jnp.int32)

    own = (me_ctx * split + me_head) * own_blocks
    base = (me_ctx - HOPS) * group
    blocks = lax.dynamic_slice_in_dim(stored_order, own, own_blocks, 0) - base
    place = blocks[:, None] * bt + jnp.arange(bt, dtype=jnp.int32)[None, :]
    ends = jnp.cumsum(doc_lengths).astype(jnp.int32) - base * bt
    start = jnp.max(
        jnp.where(ends[None, None, :] <= place[..., None], ends[None, None, :], -base * bt), axis=-1
    )
    tiles = (blocks - start[:, 0] // bt) // 2 + 1
    clean = (blocks - 1 + (-start[:, -1]) // bt) // 2 + 1
    clean = jnp.clip(clean, 1, tiles)
    spans = jnp.stack([blocks, tiles, clean], axis=1).reshape(-1).astype(jnp.int32)
    info = jnp.repeat(jnp.stack([start, place], axis=1), share, axis=2).astype(jnp.int32)

    kv = jnp.stack([keys, values]).reshape(2, own_blocks, bt, kv_heads, HEAD_SIZE)
    kv = kv.transpose(3, 0, 1, 2, 4)
    firsts = [sum(CHUNKS[:c]) for c in range(len(CHUNKS))]

    def with_others(part):
        return jnp.concatenate([part] + [rolled(part, "head", j) for j in range(1, split)], axis=2)

    near_first = with_others(kv[: CHUNKS[0]])
    near_rest = with_others(kv[CHUNKS[0] :])
    windows = []
    for first, chunk in zip(firsts, CHUNKS):
        if first == 0:
            near = near_first
        else:
            near = near_rest[first - CHUNKS[0] : first - CHUNKS[0] + chunk]
        far = [shifted(near, "ctx", hop_index) for hop_index in range(1, HOPS + 1)]
        windows.append(jnp.concatenate([near] + far, axis=2))

    so_far = None
    sums = []
    for first, window in zip(firsts, windows):
        attended, query_grad, part = attend(
            slot_of, spans, info, queries, out_grad, window, first, so_far
        )
        so_far = (attended, query_grad)
        summed = part[:, :, :group].astype(jnp.float32)
        for hop_index in range(1, HOPS + 1):
            piece = part[:, :, hop_index * group : (hop_index + 1) * group]
            summed = summed + shifted(piece, "ctx", -hop_index).astype(jnp.float32)
        sums.append(summed.astype(jnp.bfloat16))

    def over_heads(summed):
        total = summed[:, :, :own_blocks].astype(jnp.float32)
        for j in range(1, split):
            piece = summed[:, :, j * own_blocks : (j + 1) * own_blocks]
            total = total + rolled(piece, "head", -j).astype(jnp.float32)
        return total.astype(jnp.bfloat16)

    grads = [over_heads(jnp.concatenate(sums[:-1], axis=0)), over_heads(sums[-1])]
    grad = jnp.concatenate(grads, axis=0).transpose(1, 2, 3, 0, 4)
    grad = grad.reshape(2, tokens, kv_heads, HEAD_SIZE)
    return so_far[0], so_far[1], grad[0], grad[1]


def solution(mesh):
    spec = P(("ctx", "head"), None, None)
    return jax.shard_map(
        body,
        mesh=mesh,
        in_specs=(spec, spec, spec, spec, P(), P()),
        out_specs=(spec, spec, spec, spec),
        check_vma=False,
    )
```

profile of v0, /device:TPU:10, one launch (start us, length us, event | category | flops | bytes accessed | tf_op | source)
XLA Modules:
  0.0 199.7 jit_solution(7098397091943653870)
XLA Ops:
  0.6 1.1 copy.43
  1.7 1.1 copy.44
  3.0 1.6 collective-permute-start.5
  5.6 0.7 gather_fusion
  6.9 5.4 %collective-permute-done.5 = bf16[2,2,2,128,128]{4,3,2,1,0:T(8,128)(2,1)S(1)} collective-permute-done((bf16[2,2,2,128,128]{4,3,2,1,0:T(8,128)(2,1)S(1)}, bf16[2,2,2,128,128]{4,3,2,1,0:T(8,128)(2,1)S(1)}, u32[]{:S(2)}, u32[]{:S(2)}) %collective-permute-start.5) | collective-permute-done | bytes 262176 | tf_op jit(solution)/shard_map/ppermute | solution.py:202
  12.3 0.8 pad_maximum_fusion.6
  13.1 1.9 collective-permute-start.6
  15.0 3.5 %collective-permute-start.7 = (bf16[2,2,4,128,128]{4,3,2,1,0:T(8,128)(2,1)}, bf16[2,2,4,128,128]{4,3,2,1,0:T(8,128)(2,1)}, u32[]{:S(2)}, u32[]{:S(2)}) collective-permute-start(bf16[2,2,4,128,128]{4,3,2,1,0:T(8,128)(2,1)} %pad_maximum_fusion.6), channel_id=1, source_target_pairs={{0,2},{1,3},{2,4},{3,5},{4,6},{5,7},{6,8},{7,9},{8,10},{9,11},{10,... | collective-permute-start | bytes 1572872 | tf_op jit(solution)/shard_map/ppermute | solution.py:197
  18.5 9.4 %collective-permute-done = bf16[6,2,2,128,128]{4,3,2,1,0:T(8,128)(2,1)S(1)} collective-permute-done((bf16[6,2,2,128,128]{4,3,2,1,0:T(8,128)(2,1)S(1)}, bf16[6,2,2,128,128]{4,3,2,1,0:T(8,128)(2,1)S(1)}, u32[]{:S(2)}, u32[]{:S(2)}) %collective-permute-start) | collective-permute-done | bytes 786464 | tf_op jit(solution)/shard_map/ppermute | solution.py:202
  28.1 1.9 collective-permute-start.3
  30.0 3.5 %collective-permute-start.4 = (bf16[4,2,4,128,128]{4,3,2,1,0:T(8,128)(2,1)S(1)}, bf16[4,2,4,128,128]{4,3,2,1,0:T(8,128)(2,1)}, u32[]{:S(2)}, u32[]{:S(2)}) collective-permute-start(bf16[4,2,4,128,128]{4,3,2,1,0:T(8,128)(2,1)S(1)} %pad_maximum_fusion.3), channel_id=1, source_target_pairs={{0,2},{1,3},{2,4},{3,5},{4,6},{5,7},{6,8},{7,9},{8,10},{9,11},{10,... | collective-permute-start | bytes 3145736 | tf_op jit(solution)/shard_map/ppermute | solution.py:197
  34.0 1.4 pad_maximum_fusion.2.kv_ref
  35.4 14.8 %shard_map.93 = (bf16[256,64,128]{2,1,0:T(8,128)(2,1)}, bf16[256,64,128]{2,1,0:T(8,128)(2,1)}, bf16[2,2,12,128,128]{4,3,2,1,0:T(8,128)(2,1)S(1)}) custom-call(s32[12]{0:T(128)S(1)} %select_reduce_fusion.1.slot_ref, s32[6]{0:T(128)S(1)} %reshape.294.span_ref, s32[2,2,1024]{2,1,0:T(2,128)S(1)} %reshape.295.info_ref, bf16[256,64,128]{2,1,0:T(8,128)(2,1)} %q_ref.5, ...), custom_call_target="tpu_custom_call" | custom-call | flops 4831838208 | bytes 7340032 | tf_op jit(solution)/shard_map/pallas_call | solution.py:171
  50.2 0.9 fusion.16
  51.1 6.4 %collective-permute-start.8 = (bf16[2,2,4,128,128]{4,3,2,1,0:T(8,128)(2,1)}, bf16[2,2,4,128,128]{4,3,2,1,0:T(8,128)(2,1)S(1)}, u32[]{:S(2)}, u32[]{:S(2)}) collective-permute-start(bf16[2,2,4,128,128]{4,3,2,1,0:T(8,128)(2,1)} %get-tuple-element.50), channel_id=1, source_target_pairs={{1,0},{2,1},{3,2},{4,3},{5,4},{6,5},{7,6},{8,7},{9,8},{10,9},{11,1... | collective-permute-start | bytes 1572872 | tf_op jit(solution)/shard_map/ppermute | solution.py:197
  57.4 2.9 %collective-permute-start.9 = (bf16[2,2,4,128,128]{4,3,2,1,0:T(8,128)(2,1)S(1)}, bf16[2,2,4,128,128]{4,3,2,1,0:T(8,128)(2,1)S(1)}, u32[]{:S(2)}, u32[]{:S(2)}) collective-permute-start(bf16[2,2,4,128,128]{4,3,2,1,0:T(8,128)(2,1)S(1)} %get-tuple-element.51), channel_id=1, source_target_pairs={{2,0},{3,1},{4,2},{5,3},{6,4},{7,5},{8,6},{9,7},{10,8},{11,9},{12,... | collective-permute-start | bytes 1572872 | tf_op jit(solution)/shard_map/ppermute | solution.py:197
  60.4 2.1 %collective-permute-start.1 = (bf16[2,2,4,128,128]{4,3,2,1,0:T(8,128)(2,1)S(1)}, bf16[2,2,4,128,128]{4,3,2,1,0:T(8,128)(2,1)S(1)}, u32[]{:S(2)}, u32[]{:S(2)}) collective-permute-start(bf16[2,2,4,128,128]{4,3,2,1,0:T(8,128)(2,1)S(1)} %pad_maximum_fusion.5), channel_id=1, source_target_pairs={{0,1},{1,2},{2,3},{3,4},{4,5},{5,6},{6,7},{7,8},{8,9},{9,10},{10,1... | collective-permute-start | bytes 1572872 | tf_op jit(solution)/shard_map/ppermute | solution.py:197
  62.5 11.5 %collective-permute-done.3 = bf16[4,2,4,128,128]{4,3,2,1,0:T(8,128)(2,1)} collective-permute-done((bf16[4,2,4,128,128]{4,3,2,1,0:T(8,128)(2,1)S(1)}, bf16[4,2,4,128,128]{4,3,2,1,0:T(8,128)(2,1)}, u32[]{:S(2)}, u32[]{:S(2)}) %collective-permute-start.3) | collective-permute-done | bytes 1048608 | tf_op jit(solution)/shard_map/ppermute | solution.py:197
  74.0 1.9 collective-permute-start.2
  75.9 3.0 %pad_maximum_fusion.kv_ref = bf16[4,2,12,128,128]{4,3,2,1,0:T(8,128)(2,1)} fusion(bf16[4,2,4,128,128]{4,3,2,1,0:T(8,128)(2,1)} %collective-permute-done.4, bf16[4,2,4,128,128]{4,3,2,1,0:T(8,128)(2,1)} %collective-permute-done.3, bf16[4,2,4,128,128]{4,3,2,1,0:T(8,128)(2,1)S(1)} %pad_maximum_fusion.3), kind=kLoop, calls=%fused_computation.1 | loop fusion | flops 3145728 | bytes 6291456 | tf_op jit(solution)/shard_map/concatenate | solution.py:256
  78.9 27.4 %shard_map.94 = (bf16[256,64,128]{2,1,0:T(8,128)(2,1)}, bf16[256,64,128]{2,1,0:T(8,128)(2,1)}, bf16[4,2,12,128,128]{4,3,2,1,0:T(8,128)(2,1)S(1)}) custom-call(s32[12]{0:T(128)S(1)} %select_reduce_fusion.1.slot_ref, s32[6]{0:T(128)S(1)} %reshape.294.span_ref, s32[2,2,1024]{2,1,0:T(2,128)S(1)} %reshape.295.info_ref, ...), custom_call_target="tpu_custom_call", output_to_operand_aliasing={{0}: (6, {}), {1}: (7, {})} | custom-call | flops 9663676416 | bytes 14680064 | tf_op jit(solution)/shard_map/pallas_call | solution.py:171
  106.6 21.3 %collective-permute-start.10 = (bf16[4,2,4,128,128]{4,3,2,1,0:T(8,128)(2,1)S(1)}, bf16[4,2,4,128,128]{4,3,2,1,0:T(8,128)(2,1)S(1)}, u32[]{:S(2)}, u32[]{:S(2)}) collective-permute-start(bf16[4,2,4,128,128]{4,3,2,1,0:T(8,128)(2,1)S(1)} %get-tuple-element.48), channel_id=1, source_target_pairs={{1,0},{2,1},{3,2},{4,3},{5,4},{6,5},{7,6},{8,7},{9,8},{10,9},{11,1... | collective-permute-start | bytes 3145736 | tf_op jit(solution)/shard_map/ppermute | solution.py:197
  127.9 2.1 %collective-permute-start.11 = (bf16[4,2,4,128,128]{4,3,2,1,0:T(8,128)(2,1)S(1)}, bf16[4,2,4,128,128]{4,3,2,1,0:T(8,128)(2,1)S(1)}, u32[]{:S(2)}, u32[]{:S(2)}) collective-permute-start(bf16[4,2,4,128,128]{4,3,2,1,0:T(8,128)(2,1)S(1)} %get-tuple-element.49), channel_id=1, source_target_pairs={{2,0},{3,1},{4,2},{5,3},{6,4},{7,5},{8,6},{9,7},{10,8},{11,9},{12,... | collective-permute-start | bytes 3145736 | tf_op jit(solution)/shard_map/ppermute | solution.py:197
  130.2 14.8 %shard_map.95 = (bf16[256,64,128]{2,1,0:T(8,128)(2,1)}, bf16[256,64,128]{2,1,0:T(8,128)(2,1)}, bf16[2,2,12,128,128]{4,3,2,1,0:T(8,128)(2,1)S(1)}) custom-call(s32[12]{0:T(128)S(1)} %select_reduce_fusion.1.slot_ref, s32[6]{0:T(128)S(1)} %reshape.294.span_ref, s32[2,2,1024]{2,1,0:T(2,128)S(1)} %reshape.295.info_ref, ...), custom_call_target="tpu_custom_call", output_to_operand_aliasing={{0}: (6, {}), {1}: (7, {})} | custom-call | flops 4831838208 | bytes 7340032 | tf_op jit(solution)/shard_map/pallas_call | solution.py:171
  145.2 4.4 %collective-permute-start.13 = (bf16[2,2,4,128,128]{4,3,2,1,0:T(8,128)(2,1)S(1)}, bf16[2,2,4,128,128]{4,3,2,1,0:T(8,128)(2,1)S(1)}, u32[]{:S(2)}, u32[]{:S(2)}) collective-permute-start(bf16[2,2,4,128,128]{4,3,2,1,0:T(8,128)(2,1)S(1)} %get-tuple-element.52), channel_id=1, source_target_pairs={{1,0},{2,1},{3,2},{4,3},{5,4},{6,5},{7,6},{8,7},{9,8},{10,9},{11,1... | collective-permute-start | bytes 1572872 | tf_op jit(solution)/shard_map/ppermute | solution.py:197
  149.5 11.2 %collective-permute-start.14 = (bf16[2,2,4,128,128]{4,3,2,1,0:T(8,128)(2,1)S(1)}, bf16[2,2,4,128,128]{4,3,2,1,0:T(8,128)(2,1)S(1)}, u32[]{:S(2)}, u32[]{:S(2)}) collective-permute-start(bf16[2,2,4,128,128]{4,3,2,1,0:T(8,128)(2,1)S(1)} %get-tuple-element.53), channel_id=1, source_target_pairs={{2,0},{3,1},{4,2},{5,3},{6,4},{7,5},{8,6},{9,7},{10,8},{11,9},{12,... | collective-permute-start | bytes 1572872 | tf_op jit(solution)/shard_map/ppermute | solution.py:197
  161.0 3.0 %collective-permute-done.11 = bf16[4,2,4,128,128]{4,3,2,1,0:T(8,128)(2,1)S(1)} collective-permute-done((bf16[4,2,4,128,128]{4,3,2,1,0:T(8,128)(2,1)S(1)}, bf16[4,2,4,128,128]{4,3,2,1,0:T(8,128)(2,1)S(1)}, u32[]{:S(2)}, u32[]{:S(2)}) %collective-permute-start.11) | collective-permute-done | bytes 1048608 | tf_op jit(solution)/shard_map/ppermute | solution.py:197
  164.7 16.6 %collective-permute-start.12 = (bf16[6,2,2,128,128]{4,3,2,1,0:T(8,128)(2,1)S(1)}, bf16[6,2,2,128,128]{4,3,2,1,0:T(8,128)(2,1)S(1)}, u32[]{:S(2)}, u32[]{:S(2)}) collective-permute-start(bf16[6,2,2,128,128]{4,3,2,1,0:T(8,128)(2,1)S(1)} %pad_maximum_fusion.4), channel_id=1, source_target_pairs={{0,16},{16,0},{1,17},{17,1},{2,18},{18,2},{3,19},{19,3},{4,20},{20... | collective-permute-start | bytes 2359304 | tf_op jit(solution)/shard_map/ppermute | solution.py:202
  181.6 10.5 %collective-permute-start.15 = (bf16[2,2,2,128,128]{4,3,2,1,0:T(8,128)(2,1)S(1)}, bf16[2,2,2,128,128]{4,3,2,1,0:T(8,128)(2,1)S(1)}, u32[]{:S(2)}, u32[]{:S(2)}) collective-permute-start(bf16[2,2,2,128,128]{4,3,2,1,0:T(8,128)(2,1)S(1)} %slice.93), channel_id=1, source_target_pairs={{0,16},{16,0},{1,17},{17,1},{2,18},{18,2},{3,19},{19,3},{4,20},{20... | collective-permute-start | bytes 786440 | tf_op jit(solution)/shard_map/ppermute | solution.py:202
  192.1 4.8 %collective-permute-done.15 = bf16[2,2,2,128,128]{4,3,2,1,0:T(8,128)(2,1)S(1)} collective-permute-done((bf16[2,2,2,128,128]{4,3,2,1,0:T(8,128)(2,1)S(1)}, bf16[2,2,2,128,128]{4,3,2,1,0:T(8,128)(2,1)S(1)}, u32[]{:S(2)}, u32[]{:S(2)}) %collective-permute-start.15) | collective-permute-done | bytes 262176 | tf_op jit(solution)/shard_map/ppermute | solution.py:202
  197.5 1.1 copy.45
  198.6 1.1 copy.46
  (52 shorter events, 4.5 us)
Async XLA Ops:
  3.0 2.3 %copy-start = (s32[64]{0:T(128)S(1)}, s32[64]{0:T(128)}, u32[]{:S(2)}) copy-start(s32[64]{0:T(128)} %param.11) | copy-start | bytes 772
  3.0 2.4 %copy-start.1 = (s32[48]{0:T(128)S(1)}, s32[48]{0:T(128)}, u32[]{:S(2)}) copy-start(s32[48]{0:T(128)} %param.10) | copy-start | bytes 580
  3.0 9.3 %collective-permute-start.5 = (bf16[2,2,2,128,128]{4,3,2,1,0:T(8,128)(2,1)S(1)}, bf16[2,2,2,128,128]{4,3,2,1,0:T(8,128)(2,1)S(1)}, u32[]{:S(2)}, u32[]{:S(2)}) collective-permute-start(bf16[2,2,2,128,128]{4,3,2,1,0:T(8,128)(2,1)S(1)} %slice.89), channel_id=1, source_target_pairs={{0,16},{16,0},{1,17},{17,1},{2,18},{18,2},{3,19},{19,3},{4,20},{20... | collective-permute-start | bytes 786440 | tf_op jit(solution)/shard_map/ppermute | solution.py:202
  4.7 23.3 %collective-permute-start = (bf16[6,2,2,128,128]{4,3,2,1,0:T(8,128)(2,1)S(1)}, bf16[6,2,2,128,128]{4,3,2,1,0:T(8,128)(2,1)S(1)}, u32[]{:S(2)}, u32[]{:S(2)}) collective-permute-start(bf16[6,2,2,128,128]{4,3,2,1,0:T(8,128)(2,1)S(1)} %slice.88), channel_id=1, source_target_pairs={{0,16},{16,0},{1,17},{17,1},{2,18},{18,2},{3,19},{19,3},{4,20},{20... | collective-permute-start | bytes 2359304 | tf_op jit(solution)/shard_map/ppermute | solution.py:202
  13.1 20.8 %collective-permute-start.6 = (bf16[2,2,4,128,128]{4,3,2,1,0:T(8,128)(2,1)}, bf16[2,2,4,128,128]{4,3,2,1,0:T(8,128)(2,1)}, u32[]{:S(2)}, u32[]{:S(2)}) collective-permute-start(bf16[2,2,4,128,128]{4,3,2,1,0:T(8,128)(2,1)} %pad_maximum_fusion.6), channel_id=1, source_target_pairs={{0,1},{1,2},{2,3},{3,4},{4,5},{5,6},{6,7},{7,8},{8,9},{9,10},{10,1... | collective-permute-start | bytes 1572872 | tf_op jit(solution)/shard_map/ppermute | solution.py:197
  15.0 18.9 %collective-permute-start.7 = (bf16[2,2,4,128,128]{4,3,2,1,0:T(8,128)(2,1)}, bf16[2,2,4,128,128]{4,3,2,1,0:T(8,128)(2,1)}, u32[]{:S(2)}, u32[]{:S(2)}) collective-permute-start(bf16[2,2,4,128,128]{4,3,2,1,0:T(8,128)(2,1)} %pad_maximum_fusion.6), channel_id=1, source_target_pairs={{0,2},{1,3},{2,4},{3,5},{4,6},{5,7},{6,8},{7,9},{8,10},{9,11},{10,... | collective-permute-start | bytes 1572872 | tf_op jit(solution)/shard_map/ppermute | solution.py:197
  28.1 45.9 %collective-permute-start.3 = (bf16[4,2,4,128,128]{4,3,2,1,0:T(8,128)(2,1)S(1)}, bf16[4,2,4,128,128]{4,3,2,1,0:T(8,128)(2,1)}, u32[]{:S(2)}, u32[]{:S(2)}) collective-permute-start(bf16[4,2,4,128,128]{4,3,2,1,0:T(8,128)(2,1)S(1)} %pad_maximum_fusion.3), channel_id=1, source_target_pairs={{0,1},{1,2},{2,3},{3,4},{4,5},{5,6},{6,7},{7,8},{8,9},{9,10},{10,1... | collective-permute-start | bytes 3145736 | tf_op jit(solution)/shard_map/ppermute | solution.py:197
  30.0 45.9 %collective-permute-start.4 = (bf16[4,2,4,128,128]{4,3,2,1,0:T(8,128)(2,1)S(1)}, bf16[4,2,4,128,128]{4,3,2,1,0:T(8,128)(2,1)}, u32[]{:S(2)}, u32[]{:S(2)}) collective-permute-start(bf16[4,2,4,128,128]{4,3,2,1,0:T(8,128)(2,1)S(1)} %pad_maximum_fusion.3), channel_id=1, source_target_pairs={{0,2},{1,3},{2,4},{3,5},{4,6},{5,7},{6,8},{7,9},{8,10},{9,11},{10,... | collective-permute-start | bytes 3145736 | tf_op jit(solution)/shard_map/ppermute | solution.py:197
  51.1 98.5 %collective-permute-start.8 = (bf16[2,2,4,128,128]{4,3,2,1,0:T(8,128)(2,1)}, bf16[2,2,4,128,128]{4,3,2,1,0:T(8,128)(2,1)S(1)}, u32[]{:S(2)}, u32[]{:S(2)}) collective-permute-start(bf16[2,2,4,128,128]{4,3,2,1,0:T(8,128)(2,1)} %get-tuple-element.50), channel_id=1, source_target_pairs={{1,0},{2,1},{3,2},{4,3},{5,4},{6,5},{7,6},{8,7},{9,8},{10,9},{11,1... | collective-permute-start | bytes 1572872 | tf_op jit(solution)/shard_map/ppermute | solution.py:197
  57.4 103.3 %collective-permute-start.9 = (bf16[2,2,4,128,128]{4,3,2,1,0:T(8,128)(2,1)S(1)}, bf16[2,2,4,128,128]{4,3,2,1,0:T(8,128)(2,1)S(1)}, u32[]{:S(2)}, u32[]{:S(2)}) collective-permute-start(bf16[2,2,4,128,128]{4,3,2,1,0:T(8,128)(2,1)S(1)} %get-tuple-element.51), channel_id=1, source_target_pairs={{2,0},{3,1},{4,2},{5,3},{6,4},{7,5},{8,6},{9,7},{10,8},{11,9},{12,... | collective-permute-start | bytes 1572872 | tf_op jit(solution)/shard_map/ppermute | solution.py:197
  60.4 67.6 %collective-permute-start.1 = (bf16[2,2,4,128,128]{4,3,2,1,0:T(8,128)(2,1)S(1)}, bf16[2,2,4,128,128]{4,3,2,1,0:T(8,128)(2,1)S(1)}, u32[]{:S(2)}, u32[]{:S(2)}) collective-permute-start(bf16[2,2,4,128,128]{4,3,2,1,0:T(8,128)(2,1)S(1)} %pad_maximum_fusion.5), channel_id=1, source_target_pairs={{0,1},{1,2},{2,3},{3,4},{4,5},{5,6},{6,7},{7,8},{8,9},{9,10},{10,1... | collective-permute-start | bytes 1572872 | tf_op jit(solution)/shard_map/ppermute | solution.py:197
  74.0 56.1 %collective-permute-start.2 = (bf16[2,2,4,128,128]{4,3,2,1,0:T(8,128)(2,1)S(1)}, bf16[2,2,4,128,128]{4,3,2,1,0:T(8,128)(2,1)S(1)}, u32[]{:S(2)}, u32[]{:S(2)}) collective-permute-start(bf16[2,2,4,128,128]{4,3,2,1,0:T(8,128)(2,1)S(1)} %pad_maximum_fusion.5), channel_id=1, source_target_pairs={{0,2},{1,3},{2,4},{3,5},{4,6},{5,7},{6,8},{7,9},{8,10},{9,11},{10,... | collective-permute-start | bytes 1572872 | tf_op jit(solution)/shard_map/ppermute | solution.py:197
  106.6 54.4 %collective-permute-start.10 = (bf16[4,2,4,128,128]{4,3,2,1,0:T(8,128)(2,1)S(1)}, bf16[4,2,4,128,128]{4,3,2,1,0:T(8,128)(2,1)S(1)}, u32[]{:S(2)}, u32[]{:S(2)}) collective-permute-start(bf16[4,2,4,128,128]{4,3,2,1,0:T(8,128)(2,1)S(1)} %get-tuple-element.48), channel_id=1, source_target_pairs={{1,0},{2,1},{3,2},{4,3},{5,4},{6,5},{7,6},{8,7},{9,8},{10,9},{11,1... | collective-permute-start | bytes 3145736 | tf_op jit(solution)/shard_map/ppermute | solution.py:197
  127.9 36.0 %collective-permute-start.11 = (bf16[4,2,4,128,128]{4,3,2,1,0:T(8,128)(2,1)S(1)}, bf16[4,2,4,128,128]{4,3,2,1,0:T(8,128)(2,1)S(1)}, u32[]{:S(2)}, u32[]{:S(2)}) collective-permute-start(bf16[4,2,4,128,128]{4,3,2,1,0:T(8,128)(2,1)S(1)} %get-tuple-element.49), channel_id=1, source_target_pairs={{2,0},{3,1},{4,2},{5,3},{6,4},{7,5},{8,6},{9,7},{10,8},{11,9},{12,... | collective-permute-start | bytes 3145736 | tf_op jit(solution)/shard_map/ppermute | solution.py:197
  145.2 36.2 %collective-permute-start.13 = (bf16[2,2,4,128,128]{4,3,2,1,0:T(8,128)(2,1)S(1)}, bf16[2,2,4,128,128]{4,3,2,1,0:T(8,128)(2,1)S(1)}, u32[]{:S(2)}, u32[]{:S(2)}) collective-permute-start(bf16[2,2,4,128,128]{4,3,2,1,0:T(8,128)(2,1)S(1)} %get-tuple-element.52), channel_id=1, source_target_pairs={{1,0},{2,1},{3,2},{4,3},{5,4},{6,5},{7,6},{8,7},{9,8},{10,9},{11,1... | collective-permute-start | bytes 1572872 | tf_op jit(solution)/shard_map/ppermute | solution.py:197
  149.5 31.8 %collective-permute-start.14 = (bf16[2,2,4,128,128]{4,3,2,1,0:T(8,128)(2,1)S(1)}, bf16[2,2,4,128,128]{4,3,2,1,0:T(8,128)(2,1)S(1)}, u32[]{:S(2)}, u32[]{:S(2)}) collective-permute-start(bf16[2,2,4,128,128]{4,3,2,1,0:T(8,128)(2,1)S(1)} %get-tuple-element.53), channel_id=1, source_target_pairs={{2,0},{3,1},{4,2},{5,3},{6,4},{7,5},{8,6},{9,7},{10,8},{11,9},{12,... | collective-permute-start | bytes 1572872 | tf_op jit(solution)/shard_map/ppermute | solution.py:197
  164.7 32.3 %collective-permute-start.12 = (bf16[6,2,2,128,128]{4,3,2,1,0:T(8,128)(2,1)S(1)}, bf16[6,2,2,128,128]{4,3,2,1,0:T(8,128)(2,1)S(1)}, u32[]{:S(2)}, u32[]{:S(2)}) collective-permute-start(bf16[6,2,2,128,128]{4,3,2,1,0:T(8,128)(2,1)S(1)} %pad_maximum_fusion.4), channel_id=1, source_target_pairs={{0,16},{16,0},{1,17},{17,1},{2,18},{18,2},{3,19},{19,3},{4,20},{20... | collective-permute-start | bytes 2359304 | tf_op jit(solution)/shard_map/ppermute | solution.py:202
  181.6 15.3 %collective-permute-start.15 = (bf16[2,2,2,128,128]{4,3,2,1,0:T(8,128)(2,1)S(1)}, bf16[2,2,2,128,128]{4,3,2,1,0:T(8,128)(2,1)S(1)}, u32[]{:S(2)}, u32[]{:S(2)}) collective-permute-start(bf16[2,2,2,128,128]{4,3,2,1,0:T(8,128)(2,1)S(1)} %slice.93), channel_id=1, source_target_pairs={{0,16},{16,0},{1,17},{17,1},{2,18},{18,2},{3,19},{19,3},{4,20},{20... | collective-permute-start | bytes 786440 | tf_op jit(solution)/shard_map/ppermute | solution.py:202
where the time goes:
time: 201 us; the launch traced here: 200 us
  starting transfers between devices  92.3 us (46%)
  Pallas kernels  57 us (28%)
  waiting for transfers between devices  34.2 us (17%)
  other arithmetic  7.91 us (4%)
  local copies, waits for them, and re-layouts  7.27 us (4%)
    ppermute x12, starting transfers between devices, shifted(): return lax.ppermute(block, axis, route)  63 us
    pallas_call x3, Pallas kernels, attend(): pl.pallas_call(attention_kernel, grid_spec=pltpu.PrefetchScalarGridSpec(n...  57 us
    ppermute x4, starting transfers between devices, rolled(): lax.ppermute(block, axis, [(i, (i + distance) % size) for i in range(size)])  29.3 us
    ppermute x4, waiting for transfers between devices, rolled(): lax.ppermute(block, axis, [(i, (i + distance) % size) for i in range(size)])  19.7 us
    ppermute x12, waiting for transfers between devices, shifted(): return lax.ppermute(block, axis, route)  14.5 us
    concatenate x3, other arithmetic, body(): windows.append(jnp.concatenate([near] + far, axis=2))  4.57 us
    unnamed x8, local copies, waits for them, and re-layouts  4.51 us
  transfers between devices with their start and end apart: 16, of which 5 were waited for; matrix products, arithmetic and copies ran while one was open for 5% of the time, Pallas kernels for 29%

commit v1 on v0

v1 whole, which is shorter than its diff:
```python
import functools
import math

import jax
import jax.numpy as jnp
from jax import lax
from jax.experimental import pallas as pl
from jax.experimental.pallas import tpu as pltpu
from jax.sharding import PartitionSpec as P

HEAD_SIZE = 128
BLOCK_TOKENS = 128
HOPS = 2
DOC_MOST = 1024
SIDE = 2
NEG_BIG = -1e30
SCALE = HEAD_SIZE ** (-0.5)
SCALE_LOG2 = SCALE * math.log2(math.e)

NN = (((1,), (0,)), ((), ()))
NT = (((1,), (1,)), ((), ()))
TN = (((0,), (0,)), ((), ()))


def dot(a, b, dims):
    return lax.dot_general(a, b, dims, preferred_element_type=jnp.float32)


def fused_kernel(tab_ref, inv_ref, info_ref, q_ref, g_ref, kv_ref, o_ref, dq_ref, dkv_ref, *scratch):
    s_scr, e_scr, out_acc, dq_acc, part, acc = (scratch[k * SIDE : (k + 1) * SIDE] for k in range(6))
    near, land, stage, back_land, own, send, recv, back_send, back_recv = scratch[6 * SIDE :]
    step, turn = pl.program_id(0), pl.program_id(1)
    steps, turns = pl.num_programs(0), pl.num_programs(1)
    bt = q_ref.shape[0]
    share = q_ref.shape[1] // SIDE
    rows = bt * share
    sides = range(SIDE)
    max_tiles = s_scr[0].shape[0]
    reach = 2 * max_tiles
    own_blocks = kv_ref.shape[3]
    split, row = lax.axis_size("head"), lax.axis_size("ctx")
    me_head, me_ctx = lax.axis_index("head"), lax.axis_index("ctx")
    groups = (HOPS + 1) * split
    window_blocks = groups * own_blocks

    def ahead(g):
        return {"ctx": lax.rem(me_ctx + g // split, row), "head": lax.rem(me_head + g % split, split)}

    def behind(g):
        return {
            "ctx": lax.rem(me_ctx + row - g // split, row),
            "head": lax.rem(me_head + split - g % split, split),
        }

    def has_ahead(g):
        return me_ctx + g // split < row

    def has_behind(g):
        return me_ctx >= g // split

    def forth(g, p):
        return pltpu.make_async_remote_copy(
            src_ref=kv_ref.at[p], dst_ref=land.at[p, g - 1],
            send_sem=send.at[p, g - 1], recv_sem=recv.at[p, g - 1],
            device_id=ahead(g), device_id_type=pl.DeviceIdType.MESH,
        )

    def home(g, p):
        return pltpu.make_async_remote_copy(
            src_ref=stage.at[p, g - 1], dst_ref=back_land.at[p, g - 1],
            send_sem=back_send.at[p, g - 1], recv_sem=back_recv.at[p, g - 1],
            device_id=behind(g), device_id_type=pl.DeviceIdType.MESH,
        )

    def send_forth(p):
        for g in range(1, groups):
            @pl.when(has_ahead(g))
            def _():
                forth(g, p).start()

    @pl.when((step == 0) & (turn == 0))
    def _():
        barrier = pltpu.get_barrier_semaphore()
        for g in range(1, groups):
            @pl.when(has_ahead(g))
            def _():
                pl.semaphore_signal(
                    barrier, inc=1, device_id=ahead(g), device_id_type=pl.DeviceIdType.MESH
                )

            if g >= split:
                @pl.when(has_behind(g))
                def _():
                    pl.semaphore_signal(
                        barrier, inc=1, device_id=behind(g), device_id_type=pl.DeviceIdType.MESH
                    )

        peers = split - 1
        for d in range(1, HOPS + 1):
            ends = (me_ctx + d < row).astype(jnp.int32) + (me_ctx >= d).astype(jnp.int32)
            peers = peers + split * ends
        pl.semaphore_wait(barrier, peers)

        send_forth(0)
        for a in sides:
            part[a][:, reach] = jnp.zeros((2, bt, HEAD_SIZE), jnp.float32)

    @pl.when(turn == 0)
    def _():
        for a in sides:
            near[a, :, :own_blocks] = kv_ref[step, a]
        for g in range(1, groups):
            place_of = slice(g * own_blocks, (g + 1) * own_blocks)

            @pl.when(has_behind(g))
            def _():
                forth(g, step).wait_recv()
                near[:, :, place_of] = land[step, g - 1]

            @pl.when(jnp.logical_not(has_behind(g)))
            def _():
                near[:, :, place_of] = jnp.zeros((SIDE, 2, own_blocks, bt, HEAD_SIZE), jnp.bfloat16)

        @pl.when(step + 1 < steps)
        def _():
            send_forth(step + 1)

    query = [q_ref[:, a * share : (a + 1) * share, :].reshape(rows, HEAD_SIZE) for a in sides]
    query_t = [q.T for q in query]
    start = info_ref[turn, 0:1, :]
    place = info_ref[turn, 1:2, :]

    def tile_of(a, which, t):
        low = tab_ref[turn * reach + 2 * t + 1]
        high = tab_ref[turn * reach + 2 * t]
        return jnp.concatenate([near[a, which, low], near[a, which, high]], axis=0)

    def fold(x, op):
        return op(x.reshape(2 * bt // 8, 8, rows), axis=0)

    def scores(t, upper):
        found = []
        kpos = lax.broadcasted_iota(jnp.int32, (2 * bt, 1), 0) - (2 * t + 1) * bt
        keep = kpos >= start
        if upper:
            keep = keep & (kpos <= place)
        for a in sides:
            s = dot(tile_of(a, 0, t), query_t[a], NN)
            s = jnp.where(keep, s, NEG_BIG)
            s_scr[a][t] = s
            found.append(fold(s, jnp.max))
        return found

    best = scores(0, True)
    best = lax.fori_loop(
        1, max_tiles, lambda t, m: [jnp.maximum(x, y) for x, y in zip(m, scores(t, False))], best
    )
    top = [jnp.max(m, axis=0, keepdims=True) * SCALE_LOG2 for m in best]

    for a in sides:
        out_acc[a][...] = jnp.zeros_like(out_acc[a])
        dq_acc[a][...] = jnp.zeros_like(dq_acc[a])

    def weights(t, totals):
        new = []
        for a in sides:
            e = jnp.exp2(s_scr[a][t] * SCALE_LOG2 - top[a])
            low = e.astype(jnp.bfloat16)
            e_scr[a][t] = low
            out_acc[a][...] += dot(tile_of(a, 1, t), low, TN)
            new.append(totals[a] + fold(e, jnp.sum))
        return new

    totals = lax.fori_loop(0, max_tiles, weights, [jnp.zeros((8, rows), jnp.float32)] * SIDE)
    grad_t, grad, delta = [], [], []
    for a in sides:
        inv = 1.0 / jnp.sum(totals[a], axis=0, keepdims=True)
        mine = slice(a * share, (a + 1) * share)
        out_t = (out_acc[a][...] * inv).astype(jnp.bfloat16)
        o_ref[:, mine, :] = out_t.T.reshape(bt, share, HEAD_SIZE)
        raw = g_ref[:, mine, :].reshape(rows, HEAD_SIZE).T
        scaled = (raw.astype(jnp.float32) * inv).astype(jnp.bfloat16)
        product = scaled.astype(jnp.float32) * out_t.astype(jnp.float32)
        delta.append(jnp.sum(product, axis=0, keepdims=True))
        grad_t.append(scaled)
        grad.append(scaled.T)

    def back(t, carry):
        for a in sides:
            e = e_scr[a][t]
            dp = dot(tile_of(a, 1, t), grad_t[a], NN)
            ds = (e.astype(jnp.float32) * (dp - delta[a])).astype(jnp.bfloat16)
            dq_acc[a][...] += dot(tile_of(a, 0, t), ds, TN)
            dk = dot(ds, query[a], NN)
            dv = dot(e, grad[a], NN)
            part[a][0, 2 * t + 1] = dk[:bt]
            part[a][0, 2 * t] = dk[bt:]
            part[a][1, 2 * t + 1] = dv[:bt]
            part[a][1, 2 * t] = dv[bt:]
        return carry

    lax.fori_loop(0, max_tiles, back, 0)
    for a in sides:
        mine = slice(a * share, (a + 1) * share)
        dq = (dq_acc[a][...] * SCALE).astype(jnp.bfloat16)
        dq_ref[:, mine, :] = dq.T.reshape(bt, share, HEAD_SIZE)

    @pl.when(turn == 0)
    def _():
        for a in sides:
            acc[a][...] = jnp.zeros_like(acc[a])

    for w in range(window_blocks):
        found = inv_ref[turn * window_blocks + w]
        for a in sides:
            for which in range(2):
                acc[a][which, w] += part[a][which, found]

    def finish(p):
        for g in range(1, groups):
            @pl.when(has_ahead(g))
            def _():
                home(g, p).wait_recv()
                own[p] += back_land[p, g - 1].astype(jnp.float32)
        for a in sides:
            dkv_ref[p * SIDE + a] = own[p, a].astype(jnp.bfloat16)

    @pl.when(turn == turns - 1)
    def _():
        for a in sides:
            for which in range(2):
                factor = SCALE if which == 0 else 1.0
                for g in range(1, groups):
                    piece = acc[a][which, g * own_blocks : (g + 1) * own_blocks] * factor
                    stage[step, g - 1, a, which] = piece.astype(jnp.bfloat16)
                own[step, a, which] = acc[a][which, :own_blocks] * factor
        for g in range(1, groups):
            @pl.when(has_behind(g))
            def _():
                home(g, step).start()

        @pl.when(step > 0)
        def _():
            finish(step - 1)

        @pl.when(step == steps - 1)
        def _():
            finish(step)
            for p in range(send.shape[0]):
                for g in range(1, groups):
                    @pl.when(has_ahead(g))
                    def _():
                        forth(g, p).wait_send()

                    @pl.when(has_behind(g))
                    def _():
                        home(g, p).wait_send()


def attend(table, inverse, info, queries, out_grad, kv, split):
    tokens, heads, _ = queries.shape
    steps, _, _, own_blocks, bt, _ = kv.shape
    turns = own_blocks
    rows = info.shape[2]
    share = rows // bt
    max_tiles = DOC_MOST // bt // 2 + 1
    reach = 2 * max_tiles
    groups = (HOPS + 1) * split
    window_blocks = groups * own_blocks
    by_head = pl.BlockSpec((bt, SIDE * share, HEAD_SIZE), lambda p, i: (i, p, 0))
    whole = pl.BlockSpec(memory_space=pltpu.VMEM)
    table_spec = pl.BlockSpec(memory_space=pltpu.SMEM)
    big = jax.ShapeDtypeStruct(queries.shape, jnp.bfloat16)
    pairs = steps * SIDE * turns * rows * reach * bt
    f32, low = jnp.float32, jnp.bfloat16
    piece = (SIDE, 2, own_blocks, bt, HEAD_SIZE)
    far = (steps, groups - 1) + piece
    sems = pltpu.SemaphoreType.DMA((steps, groups - 1))
    return pl.pallas_call(
        fused_kernel,
        grid=(steps, turns),
        in_specs=[table_spec, table_spec, whole, by_head, by_head, whole],
        out_specs=[by_head, by_head, whole],
        scratch_shapes=[pltpu.VMEM((max_tiles, 2 * bt, rows), f32)] * SIDE
        + [pltpu.VMEM((max_tiles, 2 * bt, rows), low)] * SIDE
        + [pltpu.VMEM((HEAD_SIZE, rows), f32)] * (2 * SIDE)
        + [pltpu.VMEM((2, reach + 1, bt, HEAD_SIZE), f32)] * SIDE
        + [pltpu.VMEM((2, window_blocks, bt, HEAD_SIZE), f32)] * SIDE
        + [
            pltpu.VMEM((SIDE, 2, window_blocks, bt, HEAD_SIZE), low),
            pltpu.VMEM(far, low),
            pltpu.VMEM(far, low),
            pltpu.VMEM(far, low),
            pltpu.VMEM((steps,) + piece, f32),
            sems,
            sems,
            sems,
            sems,
        ],
        out_shape=[big, big, jax.ShapeDtypeStruct((steps * SIDE,) + piece[1:], low)],
        compiler_params=pltpu.CompilerParams(
            collective_id=0, has_side_effects=True, vmem_limit_bytes=60 * 1024 * 1024
        ),
        cost_estimate=pl.CostEstimate(
            flops=12 * pairs * HEAD_SIZE,
            bytes_accessed=4 * queries.size * 2,
            transcendentals=pairs,
        ),
    )(table, inverse, info, queries, out_grad, kv)


def body(queries, keys, values, out_grad, doc_lengths, stored_block_order):
    tokens, heads, _ = queries.shape
    bt = min(BLOCK_TOKENS, tokens)
    pieces = BLOCK_TOKENS // bt
    stored_order = stored_block_order[:, None] * pieces + jnp.arange(pieces, dtype=jnp.int32)
    stored_order = stored_order.reshape(-1)
    kv_heads = keys.shape[1]
    share = heads // kv_heads
    own_blocks = tokens // bt
    split = lax.axis_size("head")
    me_head, me_ctx = lax.axis_index("head"), lax.axis_index("ctx")
    group = own_blocks * split
    window_blocks = (HOPS + 1) * group

    w = jnp.arange(window_blocks, dtype=jnp.int32)
    hop, turn, inner = w // group, (w % group) // own_blocks, w % own_blocks
    source = lax.rem(me_head - turn + split, split)
    stored = jnp.maximum(me_ctx - hop, 0) * group + source * own_blocks + inner
    rel = (HOPS - hop) * group + stored_order[stored] % group
    slot_of = jnp.sum(jnp.where(rel[None, :] == w[:, None], w[None, :], 0), axis=1).astype(jnp.int32)

    own = (me_ctx * split + me_head) * own_blocks
    base = (me_ctx - HOPS) * group
    blocks = lax.dynamic_slice_in_dim(stored_order, own, own_blocks, 0) - base
    place = blocks[:, None] * bt + jnp.arange(bt, dtype=jnp.int32)[None, :]
    ends = jnp.cumsum(doc_lengths).astype(jnp.int32) - base * bt
    start = jnp.max(
        jnp.where(ends[None, None, :] <= place[..., None], ends[None, None, :], -base * bt), axis=-1
    )
    reach = 2 * (DOC_MOST // bt // 2 + 1)
    back = blocks[:, None] - jnp.arange(reach, dtype=jnp.int32)[None, :]
    table = slot_of[jnp.maximum(back, 0)].reshape(-1)
    gap = blocks[:, None] - rel[None, :]
    inverse = jnp.where((gap >= 0) & (gap < reach), gap, reach).reshape(-1).astype(jnp.int32)
    first = blocks[:, None] * bt
    info = jnp.stack([start - first, place - first], axis=1)
    info = jnp.repeat(info, share, axis=2).astype(jnp.int32)

    kv = jnp.stack([keys, values]).reshape(2, own_blocks, bt, kv_heads, HEAD_SIZE)
    kv = kv.transpose(3, 0, 1, 2, 4)
    kv = kv.reshape(kv_heads // SIDE, SIDE, 2, own_blocks, bt, HEAD_SIZE)
    attended, query_grad, grad = attend(table, inverse, info, queries, out_grad, kv, split)
    grad = grad.transpose(1, 2, 3, 0, 4).reshape(2, tokens, kv_heads, HEAD_SIZE)
    return attended, query_grad, grad[0], grad[1]


def solution(mesh):
    spec = P(("ctx", "head"), None, None)
    return jax.shard_map(
        body,
        mesh=mesh,
        in_specs=(spec, spec, spec, spec, P(), P()),
        out_specs=(spec, spec, spec, spec),
        check_vma=False,
    )
```

time: 201 us -> 195 us (0.970)
  Pallas kernels: 57 us -> 175 us
  starting transfers between devices: 92.3 us -> 0 us
  waiting for transfers between devices: 34.2 us -> 0 us
  local copies, waits for them, and re-layouts: 7.27 us -> 16 us
  other arithmetic: 7.91 us -> 3.06 us
    pallas_call x3 -> x1, Pallas kernels: 57 us -> 175 us  [attend(): pl.pallas_call(fused_kernel, grid=(steps, turns), in_specs=[table_spec, t...]
    ppermute x16 -> x0, starting transfers between devices: 92.3 us -> none  [the longest x12 63 us: shifted(): return lax.ppermute(block, axis, route)]
    ppermute x16 -> x0, waiting for transfers between devices: 34.2 us -> none  [the longest x4 19.7 us: rolled(): lax.ppermute(block, axis, [(i, (i + distance) % size) for i in range(size)])]
    concatenate x6 -> x0, other arithmetic: 5.57 us -> none  [the longest x3 4.57 us: body(): windows.append(jnp.concatenate([near] + far, axis=2))]
    unnamed x8, local copies, waits for them, and re-layouts: 4.51 us -> 7.99 us
    another operation x2 -> x5, local copies, waits for them, and re-layouts: 0.18 us -> 3.02 us  [the longest x2 2.27 us: body(): jnp.stack([keys, values]).reshape(2, own_blocks, bt, kv_heads, HEAD_SIZE)]
  transfers between devices with their start and end apart: 16 -> 0, of which waited for: 5 -> 0; matrix products, arithmetic and copies ran while one was open for 5% -> 0% of each run, Pallas kernels for 29% -> 0%
where the time goes in v1:
time: 195 us
  Pallas kernels  175 us (90%)
  local copies, waits for them, and re-layouts  16 us (8%)
  other arithmetic  3.06 us (2%)
    pallas_call x1, Pallas kernels, attend(): pl.pallas_call(fused_kernel, grid=(steps, turns), in_specs=[table_spec, t...  175 us
    unnamed x8, local copies, waits for them, and re-layouts  7.99 us

profile of v1, /device:TPU:10, one launch (start us, length us, event | category | flops | bytes accessed | tf_op | source)
XLA Modules:
  0.0 194.8 jit_solution(15060864377525597924)
XLA Ops:
  0.7 0.7 broadcast_multiply_fusion
  1.4 0.1 iota_add_fusion
  1.5 0.1 subtract_maximum_fusion
  1.5 0.1 reshape.346
  1.7 1.3 gather_fusion
  3.0 0.1 broadcast_subtract_fusion
  3.1 0.1 sub.135
  3.1 0.5 and_select_fusion.inv_ref
  3.7 0.1 select_reduce_fusion.1
  3.8 1.2 gather_fusion.1
  5.0 0.7 copy.20
  5.7 0.1 reduce-window.8
  5.8 0.1 subtract_reduce_fusion
  5.9 0.1 select_reduce_fusion
  6.0 0.1 bitcast_subtract_fusion
  6.1 0.1 broadcast_in_dim.28
  6.2 0.8 reshape.334.info_ref
  7.0 1.1 copy.22
  8.2 1.1 copy.23
  9.3 1.1 pad_maximum_fusion
  10.4 175.0 %shard_map.93 = (bf16[256,64,128]{2,1,0:T(8,128)(2,1)}, bf16[256,64,128]{2,1,0:T(8,128)(2,1)}, bf16[8,2,2,128,128]{4,3,2,1,0:T(8,128)(2,1)}) custom-call(s32[20]{0:T(128)} %gather_fusion.1, s32[24]{0:T(128)} %and_select_fusion.inv_ref, s32[2,2,1024]{2,1,0:T(2,128)} %reshape.334.info_ref, bf16[256,64,128]{2,1,0:T(8,128)(2,1)} %q_ref.1, ...), custom_call_target="tpu_custom_call" | custom-call | flops 32212254720 | bytes 16777216 | tf_op jit(solution)/shard_map/pallas_call | solution.py:279
  185.4 0.0 copy-start.1
  185.4 1.4 fusion.12
  186.9 1.1 copy.25
  188.0 1.1 copy.24
  189.1 0.0 copy-done.1
  189.1 0.0 copy-start
  189.1 2.1 %copy.28 = bf16[256,64,128]{2,1,0:T(8,128)(2,1)} copy(bf16[256,64,128]{2,1,0:T(8,128)(2,1)S(1)} %copy-done.1) | data formatting | bytes 8388608
  191.3 1.6 copy-done
  192.8 2.0 %copy.29 = bf16[256,64,128]{2,1,0:T(8,128)(2,1)} copy(bf16[256,64,128]{2,1,0:T(8,128)(2,1)S(1)} %copy-done) | data formatting | bytes 8388608
  (7 shorter events, 0.1 us)
Async XLA Ops:
  185.4 3.7 %copy-start.1 = (bf16[256,64,128]{2,1,0:T(8,128)(2,1)S(1)}, bf16[256,64,128]{2,1,0:T(8,128)(2,1)}, u32[]{:S(2)}) copy-start(bf16[256,64,128]{2,1,0:T(8,128)(2,1)} %get-tuple-element.30) | copy-start | bytes 12582916
  189.1 3.7 %copy-start = (bf16[256,64,128]{2,1,0:T(8,128)(2,1)S(1)}, bf16[256,64,128]{2,1,0:T(8,128)(2,1)}, u32[]{:S(2)}) copy-start(bf16[256,64,128]{2,1,0:T(8,128)(2,1)} %get-tuple-element.31) | copy-start | bytes 12582916

commit v2 on v1

--- a/solution.py
+++ b/solution.py
@@ -28,7 +28,8 @@
 
 def fused_kernel(tab_ref, inv_ref, info_ref, q_ref, g_ref, kv_ref, o_ref, dq_ref, dkv_ref, *scratch):
     s_scr, e_scr, out_acc, dq_acc, part, acc = (scratch[k * SIDE : (k + 1) * SIDE] for k in range(6))
-    near, land, stage, back_land, own, send, recv, back_send, back_recv = scratch[6 * SIDE :]
+    near, land, stage, back_land, mate_land, own = scratch[6 * SIDE : 6 * SIDE + 6]
+    send, recv, pass_send, back_send, back_recv, mate_send, mate_recv = scratch[6 * SIDE + 6 :]
     step, turn = pl.program_id(0), pl.program_id(1)
     steps, turns = pl.num_programs(0), pl.num_programs(1)
     bt = q_ref.shape[0]
@@ -42,6 +43,9 @@
     me_head, me_ctx = lax.axis_index("head"), lax.axis_index("ctx")
     groups = (HOPS + 1) * split
     window_blocks = groups * own_blocks
+    even = lax.rem(me_ctx, 2) == 0
+    odd = jnp.logical_not(even)
+    mesh_ids = pl.DeviceIdType.MESH
 
     def ahead(g):
         return {"ctx": lax.rem(me_ctx + g // split, row), "head": lax.rem(me_head + g % split, split)}
@@ -72,11 +76,69 @@
             device_id=behind(g), device_id_type=pl.DeviceIdType.MESH,
         )
 
+    def passed(g, p):
+        source = kv_ref.at[p] if g == split else land.at[p, g - split - 1]
+        return pltpu.make_async_remote_copy(
+            src_ref=source, dst_ref=land.at[p, g - 1],
+            send_sem=pass_send.at[p, g - 1], recv_sem=recv.at[p, g - 1],
+            device_id={"ctx": lax.rem(me_ctx + 1, row), "head": me_head}, device_id_type=mesh_ids,
+        )
+
+    def to_mate(g, p):
+        return pltpu.make_async_remote_copy(
+            src_ref=stage.at[p, g - 1], dst_ref=mate_land.at[p, g - 1],
+            send_sem=mate_send.at[p, g - 1], recv_sem=mate_recv.at[p, g - 1],
+            device_id={"ctx": lax.rem(me_ctx + row - 1, row), "head": me_head},
+            device_id_type=mesh_ids,
+        )
+
+    def sends_forth(g):
+        return has_ahead(g) if g < split else has_ahead(g) & (lax.rem(me_ctx + g // split, 2) == 0)
+
+    def sends_home(g):
+        return has_behind(g) if g < split else has_behind(g) & even
+
+    def passes(g):
+        return even & has_behind(g - split)
+
     def send_forth(p):
         for g in range(1, groups):
-            @pl.when(has_ahead(g))
+            @pl.when(sends_forth(g))
             def _():
                 forth(g, p).start()
+
+        @pl.when(even)
+        def _():
+            passed(split, p).start()
+
+    def arrive(p):
+        for g in range(1, groups):
+            @pl.when(has_behind(g))
+            def _():
+                forth(g, p).wait_recv()
+
+    def pass_on(p):
+        @pl.when(even)
+        def _():
+            arrive(p)
+        for g in range(split + 1, groups):
+            @pl.when(passes(g))
+            def _():
+                passed(g, p).start()
+
+    def settle(p):
+        for g in range(groups - split):
+            @pl.when(even & has_behind(g))
+            def _():
+                to_mate(g + split, p).wait_recv()
+                other = mate_land[p, g + split - 1].astype(jnp.float32)
+                if g == 0:
+                    own[p] += other
+                else:
+                    stage[p, g - 1] = (stage[p, g - 1].astype(jnp.float32) + other).astype(
+                        jnp.bfloat16
+                    )
+                    home(g, p).start()
 
     @pl.when((step == 0) & (turn == 0))
     def _():
@@ -102,11 +164,15 @@
         pl.semaphore_wait(barrier, peers)
 
         send_forth(0)
+        pass_on(0)
         for a in sides:
             part[a][:, reach] = jnp.zeros((2, bt, HEAD_SIZE), jnp.float32)
 
     @pl.when(turn == 0)
     def _():
+        @pl.when(odd)
+        def _():
+            arrive(step)
         for a in sides:
             near[a, :, :own_blocks] = kv_ref[step, a]
         for g in range(1, groups):
@@ -114,16 +180,29 @@
 
             @pl.when(has_behind(g))
             def _():
-                forth(g, step).wait_recv()
                 near[:, :, place_of] = land[step, g - 1]
 
             @pl.when(jnp.logical_not(has_behind(g)))
             def _():
                 near[:, :, place_of] = jnp.zeros((SIDE, 2, own_blocks, bt, HEAD_SIZE), jnp.bfloat16)
 
+        @pl.when(step == 0)
+        def _():
+            send_forth(1)
+
+    @pl.when(turn == turns - 1)
+    def _():
         @pl.when(step + 1 < steps)
         def _():
-            send_forth(step + 1)
+            pass_on(step + 1)
+
+        @pl.when(step + 2 < steps)
+        def _():
+            send_forth(step + 2)
+
+        @pl.when(step > 0)
+        def _():
+            settle(step - 1)
 
     query = [q_ref[:, a * share : (a + 1) * share, :].reshape(rows, HEAD_SIZE) for a in sides]
     query_t = [q.T for q in query]
@@ -218,7 +297,11 @@
 
     def finish(p):
         for g in range(1, groups):
-            @pl.when(has_ahead(g))
+            comes = has_ahead(g)
+            if g >= split:
+                comes = comes & (lax.rem(me_ctx + g // split, 2) == 0)
+
+            @pl.when(comes)
             def _():
                 home(g, p).wait_recv()
                 own[p] += back_land[p, g - 1].astype(jnp.float32)
@@ -235,26 +318,42 @@
                     stage[step, g - 1, a, which] = piece.astype(jnp.bfloat16)
                 own[step, a, which] = acc[a][which, :own_blocks] * factor
         for g in range(1, groups):
-            @pl.when(has_behind(g))
+            if g >= split:
+                @pl.when(odd & has_behind(g))
+                def _():
+                    to_mate(g, step).start()
+
+            @pl.when((even if g >= groups - split else odd) & sends_home(g))
             def _():
                 home(g, step).start()
 
-        @pl.when(step > 0)
-        def _():
+        @pl.when(step > 1)
+        def _():
+            finish(step - 2)
+
+        @pl.when(step == steps - 1)
+        def _():
+            settle(step)
             finish(step - 1)
-
-        @pl.when(step == steps - 1)
-        def _():
             finish(step)
             for p in range(send.shape[0]):
                 for g in range(1, groups):
-                    @pl.when(has_ahead(g))
+                    @pl.when(sends_forth(g))
                     def _():
                         forth(g, p).wait_send()
 
-                    @pl.when(has_behind(g))
+                    @pl.when(sends_home(g))
                     def _():
                         home(g, p).wait_send()
+
+                    if g >= split:
+                        @pl.when(passes(g))
+                        def _():
+                            passed(g, p).wait_send()
+
+                        @pl.when(odd & has_behind(g))
+                        def _():
+                            to_mate(g, p).wait_send()
 
 
 def attend(table, inverse, info, queries, out_grad, kv, split):
@@ -291,7 +390,11 @@
             pltpu.VMEM(far, low),
             pltpu.VMEM(far, low),
             pltpu.VMEM(far, low),
+            pltpu.VMEM(far, low),
             pltpu.VMEM((steps,) + piece, f32),
+            sems,
+            sems,
+            sems,
             sems,
             sems,
             sems,

time: 195 us -> 173 us (0.89)
  the two profiles are of different devices: /device:TPU:10 before, /device:TPU:1 now
where the time goes in v2:
time: 173 us
  Pallas kernels  153 us (88%)
  local copies, waits for them, and re-layouts  16 us (9%)
  other arithmetic  3.06 us (2%)
    pallas_call x1, Pallas kernels, attend(): pl.pallas_call(fused_kernel, grid=(steps, turns), in_specs=[table_spec, t...  153 us
    unnamed x8, local copies, waits for them, and re-layouts  7.99 us

profile of v2, /device:TPU:1, one launch (start us, length us, event | category | flops | bytes accessed | tf_op | source)
XLA Modules:
  0.0 173.2 jit_solution(2470606380760796657)
XLA Ops:
  0.7 0.7 broadcast_multiply_fusion
  1.4 0.1 iota_add_fusion
  1.5 0.1 subtract_maximum_fusion
  1.5 0.1 reshape.346
  1.7 1.3 gather_fusion
  3.0 0.1 broadcast_subtract_fusion
  3.1 0.1 sub.135
  3.1 0.5 and_select_fusion.inv_ref
  3.7 0.1 select_reduce_fusion.1
  3.8 1.2 gather_fusion.1
  5.0 0.7 copy.20
  5.7 0.1 reduce-window.8
  5.8 0.1 subtract_reduce_fusion
  5.9 0.1 select_reduce_fusion
  6.0 0.1 bitcast_subtract_fusion
  6.1 0.1 broadcast_in_dim.28
  6.2 0.8 reshape.334.info_ref
  7.0 1.1 copy.22
  8.2 1.1 copy.23
  9.3 1.1 pad_maximum_fusion
  10.4 153.4 %shard_map.93 = (bf16[256,64,128]{2,1,0:T(8,128)(2,1)}, bf16[256,64,128]{2,1,0:T(8,128)(2,1)}, bf16[8,2,2,128,128]{4,3,2,1,0:T(8,128)(2,1)}) custom-call(s32[20]{0:T(128)} %gather_fusion.1, s32[24]{0:T(128)} %and_select_fusion.inv_ref, s32[2,2,1024]{2,1,0:T(2,128)} %reshape.334.info_ref, bf16[256,64,128]{2,1,0:T(8,128)(2,1)} %q_ref.1, ...), custom_call_target="tpu_custom_call" | custom-call | flops 32212254720 | bytes 16777216 | tf_op jit(solution)/shard_map/pallas_call | solution.py:378
  163.8 0.0 copy-start.1
  163.8 1.4 fusion.12
  165.2 1.1 copy.25
  166.3 1.1 copy.24
  167.5 0.0 copy-done.1
  167.5 0.0 copy-start
  167.5 2.1 %copy.28 = bf16[256,64,128]{2,1,0:T(8,128)(2,1)} copy(bf16[256,64,128]{2,1,0:T(8,128)(2,1)S(1)} %copy-done.1) | data formatting | bytes 8388608
  169.6 1.6 copy-done
  171.2 2.0 %copy.29 = bf16[256,64,128]{2,1,0:T(8,128)(2,1)} copy(bf16[256,64,128]{2,1,0:T(8,128)(2,1)S(1)} %copy-done) | data formatting | bytes 8388608
  (7 shorter events, 0.1 us)
Async XLA Ops:
  163.8 3.7 %copy-start.1 = (bf16[256,64,128]{2,1,0:T(8,128)(2,1)S(1)}, bf16[256,64,128]{2,1,0:T(8,128)(2,1)}, u32[]{:S(2)}) copy-start(bf16[256,64,128]{2,1,0:T(8,128)(2,1)} %get-tuple-element.30) | copy-start | bytes 12582916
  167.5 3.7 %copy-start = (bf16[256,64,128]{2,1,0:T(8,128)(2,1)S(1)}, bf16[256,64,128]{2,1,0:T(8,128)(2,1)}, u32[]{:S(2)}) copy-start(bf16[256,64,128]{2,1,0:T(8,128)(2,1)} %get-tuple-element.31) | copy-start | bytes 12582916

commit v3 on v2

--- a/solution.py
+++ b/solution.py
@@ -27,9 +27,11 @@
 
 
 def fused_kernel(tab_ref, inv_ref, info_ref, q_ref, g_ref, kv_ref, o_ref, dq_ref, dkv_ref, *scratch):
-    s_scr, e_scr, out_acc, dq_acc, part, acc = (scratch[k * SIDE : (k + 1) * SIDE] for k in range(6))
-    near, land, stage, back_land, mate_land, own = scratch[6 * SIDE : 6 * SIDE + 6]
-    send, recv, pass_send, back_send, back_recv, mate_send, mate_recv = scratch[6 * SIDE + 6 :]
+    s_scr, e_scr, s_top, e_top, out_acc, dq_acc, part, acc = (
+        scratch[k * SIDE : (k + 1) * SIDE] for k in range(8)
+    )
+    near, land, stage, back_land, mate_land, own = scratch[8 * SIDE : 8 * SIDE + 6]
+    send, recv, pass_send, back_send, back_recv, mate_send, mate_recv = scratch[8 * SIDE + 6 :]
     step, turn = pl.program_id(0), pl.program_id(1)
     steps, turns = pl.num_programs(0), pl.num_programs(1)
     bt = q_ref.shape[0]
@@ -37,7 +39,7 @@
     rows = bt * share
     sides = range(SIDE)
     max_tiles = s_scr[0].shape[0]
-    reach = 2 * max_tiles
+    reach = 2 * max_tiles + 1
     own_blocks = kv_ref.shape[3]
     split, row = lax.axis_size("head"), lax.axis_size("ctx")
     me_head, me_ctx = lax.axis_index("head"), lax.axis_index("ctx")
@@ -210,47 +212,57 @@
     place = info_ref[turn, 1:2, :]
 
     def tile_of(a, which, t):
-        low = tab_ref[turn * reach + 2 * t + 1]
-        high = tab_ref[turn * reach + 2 * t]
+        if t is None:
+            return near[a, which, tab_ref[turn * reach]]
+        low = tab_ref[turn * reach + 2 * t + 2]
+        high = tab_ref[turn * reach + 2 * t + 1]
         return jnp.concatenate([near[a, which, low], near[a, which, high]], axis=0)
 
     def fold(x, op):
-        return op(x.reshape(2 * bt // 8, 8, rows), axis=0)
-
-    def scores(t, upper):
+        return op(x.reshape(x.shape[0] // 8, 8, rows), axis=0)
+
+    def scores(t):
         found = []
-        kpos = lax.broadcasted_iota(jnp.int32, (2 * bt, 1), 0) - (2 * t + 1) * bt
-        keep = kpos >= start
-        if upper:
-            keep = keep & (kpos <= place)
+        count = bt if t is None else 2 * bt
+        kpos = lax.broadcasted_iota(jnp.int32, (count, 1), 0)
+        if t is None:
+            keep = (kpos >= start) & (kpos <= place)
+        else:
+            keep = kpos - (2 * t + 2) * bt >= start
         for a in sides:
             s = dot(tile_of(a, 0, t), query_t[a], NN)
             s = jnp.where(keep, s, NEG_BIG)
-            s_scr[a][t] = s
+            if t is None:
+                s_top[a][...] = s
+            else:
+                s_scr[a][t] = s
             found.append(fold(s, jnp.max))
         return found
 
-    best = scores(0, True)
+    best = scores(None)
     best = lax.fori_loop(
-        1, max_tiles, lambda t, m: [jnp.maximum(x, y) for x, y in zip(m, scores(t, False))], best
+        0, max_tiles, lambda t, m: [jnp.maximum(x, y) for x, y in zip(m, scores(t))], best
     )
     top = [jnp.max(m, axis=0, keepdims=True) * SCALE_LOG2 for m in best]
 
-    for a in sides:
-        out_acc[a][...] = jnp.zeros_like(out_acc[a])
-        dq_acc[a][...] = jnp.zeros_like(dq_acc[a])
-
     def weights(t, totals):
         new = []
         for a in sides:
-            e = jnp.exp2(s_scr[a][t] * SCALE_LOG2 - top[a])
+            s = s_top[a][...] if t is None else s_scr[a][t]
+            e = jnp.exp2(s * SCALE_LOG2 - top[a])
             low = e.astype(jnp.bfloat16)
-            e_scr[a][t] = low
-            out_acc[a][...] += dot(tile_of(a, 1, t), low, TN)
-            new.append(totals[a] + fold(e, jnp.sum))
+            added = dot(tile_of(a, 1, t), low, TN)
+            if t is None:
+                e_top[a][...] = low
+                out_acc[a][...] = added
+                new.append(fold(e, jnp.sum))
+            else:
+                e_scr[a][t] = low
+                out_acc[a][...] += added
+                new.append(totals[a] + fold(e, jnp.sum))
         return new
 
-    totals = lax.fori_loop(0, max_tiles, weights, [jnp.zeros((8, rows), jnp.float32)] * SIDE)
+    totals = lax.fori_loop(0, max_tiles, weights, weights(None, None))
     grad_t, grad, delta = [], [], []
     for a in sides:
         inv = 1.0 / jnp.sum(totals[a], axis=0, keepdims=True)
@@ -266,18 +278,25 @@
 
     def back(t, carry):
         for a in sides:
-            e = e_scr[a][t]
+            e = e_top[a][...] if t is None else e_scr[a][t]
             dp = dot(tile_of(a, 1, t), grad_t[a], NN)
             ds = (e.astype(jnp.float32) * (dp - delta[a])).astype(jnp.bfloat16)
-            dq_acc[a][...] += dot(tile_of(a, 0, t), ds, TN)
+            added = dot(tile_of(a, 0, t), ds, TN)
             dk = dot(ds, query[a], NN)
             dv = dot(e, grad[a], NN)
-            part[a][0, 2 * t + 1] = dk[:bt]
-            part[a][0, 2 * t] = dk[bt:]
-            part[a][1, 2 * t + 1] = dv[:bt]
-            part[a][1, 2 * t] = dv[bt:]
+            if t is None:
+                dq_acc[a][...] = added
+                part[a][0, 0] = dk
+                part[a][1, 0] = dv
+            else:
+                dq_acc[a][...] += added
+                part[a][0, 2 * t + 2] = dk[:bt]
+                part[a][0, 2 * t + 1] = dk[bt:]
+                part[a][1, 2 * t + 2] = dv[:bt]
+                part[a][1, 2 * t + 1] = dv[bt:]
         return carry
 
+    back(None, 0)
     lax.fori_loop(0, max_tiles, back, 0)
     for a in sides:
         mine = slice(a * share, (a + 1) * share)
@@ -362,8 +381,8 @@
     turns = own_blocks
     rows = info.shape[2]
     share = rows // bt
-    max_tiles = DOC_MOST // bt // 2 + 1
-    reach = 2 * max_tiles
+    max_tiles = DOC_MOST // bt // 2
+    reach = 2 * max_tiles + 1
     groups = (HOPS + 1) * split
     window_blocks = groups * own_blocks
     by_head = pl.BlockSpec((bt, SIDE * share, HEAD_SIZE), lambda p, i: (i, p, 0))
@@ -382,6 +401,8 @@
         out_specs=[by_head, by_head, whole],
         scratch_shapes=[pltpu.VMEM((max_tiles, 2 * bt, rows), f32)] * SIDE
         + [pltpu.VMEM((max_tiles, 2 * bt, rows), low)] * SIDE
+        + [pltpu.VMEM((bt, rows), f32)] * SIDE
+        + [pltpu.VMEM((bt, rows), low)] * SIDE
         + [pltpu.VMEM((HEAD_SIZE, rows), f32)] * (2 * SIDE)
         + [pltpu.VMEM((2, reach + 1, bt, HEAD_SIZE), f32)] * SIDE
         + [pltpu.VMEM((2, window_blocks, bt, HEAD_SIZE), f32)] * SIDE
@@ -441,7 +462,7 @@
     start = jnp.max(
         jnp.where(ends[None, None, :] <= place[..., None], ends[None, None, :], -base * bt), axis=-1
     )
-    reach = 2 * (DOC_MOST // bt // 2 + 1)
+    reach = DOC_MOST // bt + 1
     back = blocks[:, None] - jnp.arange(reach, dtype=jnp.int32)[None, :]
     table = slot_of[jnp.maximum(back, 0)].reshape(-1)
     gap = blocks[:, None] - rel[None, :]

time: 173 us -> 162 us (0.936)
  the two profiles are of different devices: /device:TPU:1 before, /device:TPU:10 now
where the time goes in v3:
time: 162 us; the launch traced here: 159 us
  Pallas kernels  140 us (86%)
  local copies, waits for them, and re-layouts  16 us (10%)
  other arithmetic  3.06 us (2%)
    pallas_call x1, Pallas kernels, attend(): pl.pallas_call(fused_kernel, grid=(steps, turns), in_specs=[table_spec, t...  140 us
    unnamed x8, local copies, waits for them, and re-layouts  7.99 us

profile of v3, /device:TPU:10, one launch (start us, length us, event | category | flops | bytes accessed | tf_op | source)
XLA Modules:
  0.0 159.5 jit_solution(2484757740414163639)
XLA Ops:
  0.7 0.7 broadcast_multiply_fusion
  1.4 0.1 iota_add_fusion
  1.5 0.1 subtract_maximum_fusion
  1.5 0.1 reshape.346
  1.7 1.3 gather_fusion
  3.0 0.1 broadcast_subtract_fusion
  3.1 0.1 sub.135
  3.1 0.5 and_select_fusion.inv_ref
  3.7 0.1 select_reduce_fusion.1
  3.8 1.2 gather_fusion.1
  5.0 0.7 copy.20
  5.7 0.1 reduce-window.8
  5.8 0.1 subtract_reduce_fusion
  5.9 0.1 select_reduce_fusion
  6.0 0.1 bitcast_subtract_fusion
  6.1 0.1 broadcast_in_dim.28
  6.2 0.8 reshape.334.info_ref
  7.0 1.1 copy.22
  8.2 1.1 copy.23
  9.3 1.1 pad_maximum_fusion
  10.4 139.7 %shard_map.93 = (bf16[256,64,128]{2,1,0:T(8,128)(2,1)}, bf16[256,64,128]{2,1,0:T(8,128)(2,1)}, bf16[8,2,2,128,128]{4,3,2,1,0:T(8,128)(2,1)}) custom-call(s32[18]{0:T(128)} %gather_fusion.1, s32[24]{0:T(128)} %and_select_fusion.inv_ref, s32[2,2,1024]{2,1,0:T(2,128)} %reshape.334.info_ref, bf16[256,64,128]{2,1,0:T(8,128)(2,1)} %q_ref.1, ...), custom_call_target="tpu_custom_call" | custom-call | flops 28991029248 | bytes 16777216 | tf_op jit(solution)/shard_map/pallas_call | solution.py:397
  150.0 0.0 copy-start.1
  150.1 1.4 fusion.12
  151.5 1.1 copy.25
  152.6 1.1 copy.24
  153.8 0.0 copy-done.1
  153.8 0.0 copy-start
  153.8 2.1 %copy.28 = bf16[256,64,128]{2,1,0:T(8,128)(2,1)} copy(bf16[256,64,128]{2,1,0:T(8,128)(2,1)S(1)} %copy-done.1) | data formatting | bytes 8388608
  155.9 1.6 copy-done
  157.5 2.0 %copy.29 = bf16[256,64,128]{2,1,0:T(8,128)(2,1)} copy(bf16[256,64,128]{2,1,0:T(8,128)(2,1)S(1)} %copy-done) | data formatting | bytes 8388608
  (7 shorter events, 0.1 us)
Async XLA Ops:
  150.0 3.7 %copy-start.1 = (bf16[256,64,128]{2,1,0:T(8,128)(2,1)S(1)}, bf16[256,64,128]{2,1,0:T(8,128)(2,1)}, u32[]{:S(2)}) copy-start(bf16[256,64,128]{2,1,0:T(8,128)(2,1)} %get-tuple-element.30) | copy-start | bytes 12582916
  153.8 3.7 %copy-start = (bf16[256,64,128]{2,1,0:T(8,128)(2,1)S(1)}, bf16[256,64,128]{2,1,0:T(8,128)(2,1)}, u32[]{:S(2)}) copy-start(bf16[256,64,128]{2,1,0:T(8,128)(2,1)} %get-tuple-element.31) | copy-start | bytes 12582916
